TPU v7x, 32 devices: a whole 2x2x4 slice. The times are simulated.
32 devices in a mesh: row: 4 (over x, core), col: 8 (over z, y).
Axes of the slice: x: 2, y: 2, z: 4, core: 2. Of those that a mesh axis runs over, the one named last changes fastest.
Arguments:
- t_slab: bfloat16 [4, 2, 512, 64], P('row', None, 'col'), may hold values from -6 to 6
- w_cycle: bfloat16 [128, 16384], P('row', 'col'), may hold values from -0.5 to 0.5
Outputs:
- t_amp: bfloat16 [2048, 128], P('row', 'col')
- cycle_z: float32 [2048, 16384], P('row', 'col')
All inputs are finite; a program needn't handle non-finite values.
Results may differ from a plain program's by a relative error of at most 0.001.
Values may be sent and summed in bfloat16 or wider, within the bound.
A program may use at most 64 MiB of HBM per device.

v0:
```python
import jax
import jax.numpy as jnp
from jax import lax
from jax.sharding import PartitionSpec as P


def shards(t_slab, w_cycle):
    local_rows = jnp.transpose(t_slab[0], (1, 0, 2)).reshape(
        t_slab.shape[2], t_slab.shape[1] * t_slab.shape[3]
    )
    t_tile = lax.all_to_all(local_rows, "col", split_axis=1, concat_axis=0, tiled=True)
    t_full = lax.all_gather(t_tile, "col", axis=1, tiled=True)
    w_full = lax.all_gather(w_cycle, "row", axis=0, tiled=True)
    cycle_z = jnp.dot(t_full, w_full, preferred_element_type=jnp.float32)
    return (t_tile, cycle_z)


def solution(mesh):
    placed = (P("row", None, "col", None), P("row", "col"))
    return jax.shard_map(
        shards,
        mesh=mesh,
        in_specs=placed,
        out_specs=(P("row", "col"), P("row", "col")),
        check_vma=False,
    )
```

profile of v0, /device:TPU:0, one launch (start us, length us, event | category | flops | bytes accessed | tf_op | source)
XLA Modules:
  0.0 50.9 jit_solution(17427372366816520272)
XLA Ops:
  0.6 0.8 %copy.5 = bf16[1,2,64,64]{2,3,1,0:T(8,128)(2,1)S(1)} copy(bf16[1,2,64,64]{3,2,1,0:T(8,128)(2,1)} %param.2) | data formatting | bytes 32768 | tf_op args[0]
  1.5 0.7 %reshape.9 = bf16[8,2,512]{2,1,0:T(2,128)(2,1)} reshape(bf16[8,16,64]{2,1,0:T(8,128)(2,1)S(1)} %bitcast.14) | data formatting | bytes 32768
  2.2 7.3 %all-to-all-start = ((bf16[8,2,512]{2,1,0:T(2,128)(2,1)}), bf16[8,2,512]{2,1,0:T(2,128)(2,1)S(1)}, u32[]{:S(2)}, u32[]{:S(2)}) async-start(bf16[8,2,512]{2,1,0:T(2,128)(2,1)} %reshape.9), calls=%async_computation | async-start | bytes 32768 | tf_op jit(solution)/shard_map/all_to_all | solution.py:11
  9.5 7.4 %all_gather.7 = bf16[128,2048]{1,0:T(8,128)(2,1)S(1)} all-gather(bf16[32,2048]{1,0:T(8,128)(2,1)} %param.3), channel_id=1, replica_groups=mesh['row'=4,'col'=8] {'row'}, dimensions={0}, use_global_device_ids=true | all-gather | bytes 655360 | tf_op jit(solution)/shard_map/all_gather | solution.py:13
  16.8 0.0 all-to-all-done
  16.8 0.1 reshape.10
  17.0 0.1 all_to_all.17
  17.1 0.0 copy-start
  17.1 31.1 %all_gather.6 = bf16[512,128]{0,1:T(8,128)(2,1)S(1)} all-gather(bf16[512,16]{0,1:T(8,128)(2,1)S(1)} %all_to_all.17), channel_id=1, replica_groups=mesh['row'=4,'col'=8] {'col'}, dimensions={1}, use_global_device_ids=true | all-gather | bytes 147456 | tf_op jit(solution)/shard_map/all_gather | solution.py:12
  48.2 2.7 %fusion = f32[512,2048]{1,0:T(8,128)} fusion(bf16[512,128]{0,1:T(8,128)(2,1)S(1)} %all_gather.6, bf16[128,2048]{1,0:T(8,128)(2,1)S(1)} %all_gather.7), kind=kOutput, calls=%fused_computation.1 | convolution fusion | flops 268435456 | bytes 4849664 | tf_op jit(solution)/shard_map/dot_general | solution.py:14
  50.9 0.0 copy-done
  (2 shorter events, 0.0 us)
Async XLA Ops:
  2.2 14.7 %all-to-all-start = ((bf16[8,2,512]{2,1,0:T(2,128)(2,1)}), bf16[8,2,512]{2,1,0:T(2,128)(2,1)S(1)}, u32[]{:S(2)}, u32[]{:S(2)}) async-start(bf16[8,2,512]{2,1,0:T(2,128)(2,1)} %reshape.9), calls=%async_computation | async-start | bytes 32768 | tf_op jit(solution)/shard_map/all_to_all | solution.py:11
  17.1 33.8 %copy-start = (bf16[512,16]{0,1:T(8,128)(2,1)}, bf16[512,16]{0,1:T(8,128)(2,1)S(1)}, u32[]{:S(2)}) copy-start(bf16[512,16]{0,1:T(8,128)(2,1)S(1)} %all_to_all.17) | copy-start | bytes 49156
where the time goes:
time: 51.2 us; the launch traced here: 50.9 us
  blocking collectives  38.4 us (75%)
  starting transfers between devices  7.28 us (14%)
  matrix products  2.74 us (5%)
  local copies, waits for them, and re-layouts  1.77 us (3%)
  between operations  0.66 us (1%)
    all_gather x1, blocking collectives, shards(): t_full = lax.all_gather(t_tile, 'col', axis=1, tiled=True)  31.1 us
    all_gather x1, blocking collectives, shards(): w_full = lax.all_gather(w_cycle, 'row', axis=0, tiled=True)  7.37 us
    all_to_all x1, starting transfers between devices, shards(): lax.all_to_all(local_rows, 'col', split_axis=1, concat_axis=0, tiled=True)  7.28 us
    dot_general x1, matrix products, shards(): cycle_z = jnp.dot(t_full, w_full, preferred_element_type=jnp.float32)  2.74 us
    unnamed x5, local copies, waits for them, and re-layouts  1.65 us
  transfers between devices with their start and end apart: 1, of which 0 were waited for; matrix products, arithmetic and copies ran while one was open for 0% of the time, Pallas kernels for 0%

commit v1 on v0

v1 whole, which is shorter than its diff:
```python
import functools

import jax
import jax.numpy as jnp
from jax import lax
from jax.experimental import pallas as pl
from jax.experimental.pallas import tpu as pltpu
from jax.sharding import PartitionSpec as P

PIECES = 4
TILE = 256
CORES = 2


def gather_kernel(
    n_row, n_col, pieces, t_ref, w_ref, t_all, w_all, t_own, local_sem,
    w_chip_send, w_chip_recv, w_core_send, w_core_recv,
    t_z_send, t_z_recv, t_y_send, t_y_recv,
):
    row, col = lax.axis_index("row"), lax.axis_index("col")
    chips, core = n_row // CORES, lax.rem(row, CORES)
    chip = row // CORES
    levels, side = n_col // 2, lax.rem(col, 2)
    level = col // 2
    width = w_ref.shape[1] // pieces

    def chip_peer(k):
        return lax.rem(chip + k, chips) * CORES + core

    def level_peer(k):
        return lax.rem(level + k, levels) * 2 + side

    other_core = chip * CORES + 1 - core
    other_side = level * 2 + 1 - side

    barrier = pltpu.get_barrier_semaphore()
    peers = [{"row": chip_peer(k), "col": col} for k in range(1, chips)]
    peers.append({"row": other_core, "col": col})
    peers += [{"row": row, "col": level_peer(k)} for k in range(1, levels)]
    peers.append({"row": row, "col": other_side})
    for peer in peers:
        pl.semaphore_signal(barrier, inc=1, device_id=peer)

    t_in = pltpu.make_async_copy(t_ref, t_own, local_sem.at[0])
    t_in.start()
    w_in = pltpu.make_async_copy(w_ref, w_all.at[row], local_sem.at[1])
    w_in.start()
    t_in.wait()
    t_all[col] = jnp.concatenate(
        [t_own[0, k] for k in range(t_own.shape[1])], axis=1
    )
    pl.semaphore_wait(barrier, len(peers))

    def w_chip(k, j):
        columns = pl.ds(j * width, width)
        return pltpu.make_async_remote_copy(
            src_ref=w_ref.at[:, columns],
            dst_ref=w_all.at[row, :, columns],
            send_sem=w_chip_send.at[k, j],
            recv_sem=w_chip_recv.at[k, j],
            device_id={"row": chip_peer(k), "col": col},
        )

    def w_core(k, j):
        columns = pl.ds(j * width, width)
        slot = lax.rem(chip - k + chips, chips) * CORES + core
        source = w_ref if k == 0 else w_all.at[slot]
        return pltpu.make_async_remote_copy(
            src_ref=source.at[:, columns],
            dst_ref=w_all.at[slot, :, columns],
            send_sem=w_core_send.at[k, j],
            recv_sem=w_core_recv.at[k, j],
            device_id={"row": other_core, "col": col},
        )

    def t_z(k):
        return pltpu.make_async_remote_copy(
            src_ref=t_all.at[col],
            dst_ref=t_all.at[col],
            send_sem=t_z_send.at[k],
            recv_sem=t_z_recv.at[k],
            device_id={"row": row, "col": level_peer(k)},
        )

    def t_y(k):
        slot = lax.rem(level - k + levels, levels) * 2 + side
        return pltpu.make_async_remote_copy(
            src_ref=t_all.at[slot],
            dst_ref=t_all.at[slot],
            send_sem=t_y_send.at[k],
            recv_sem=t_y_recv.at[k],
            device_id={"row": row, "col": other_side},
        )

    w_out = [(k, j) for j in range(pieces) for k in range(1, chips)]
    t_out = list(range(1, levels))
    for k, j in w_out:
        w_chip(k, j).start()
    for k in t_out:
        t_z(k).start()
    t_y(0).start()
    for j in range(pieces):
        w_core(0, j).start()

    for step in range(max(len(w_out), len(t_out))):
        if step < len(w_out):
            w_chip(*w_out[step]).wait_recv()
            w_core(*w_out[step]).start()
        if step < len(t_out):
            t_z(t_out[step]).wait_recv()
            t_y(t_out[step]).start()

    w_in.wait()
    for k in range(levels):
        t_y(k).wait_recv()
    for k in range(chips):
        for j in range(pieces):
            w_core(k, j).wait_recv()
    for k, j in w_out:
        w_chip(k, j).wait_send()
    for k in t_out:
        t_z(k).wait_send()
    for k in range(levels):
        t_y(k).wait_send()
    for k in range(chips):
        for j in range(pieces):
            w_core(k, j).wait_send()


def product_kernel(t_ref, w_ref, amp_ref, z_ref, z_tiles, turned, amp_own, sems, amp_sem):
    col = lax.axis_index("col")
    tile = z_tiles.shape[2]
    kc = t_ref.shape[2]
    t_full = t_ref[...].reshape(-1, kc)
    copies = []
    for j in range(z_tiles.shape[0]):
        columns = pl.ds(j * tile, tile)
        z_tiles[j] = jnp.dot(
            t_full,
            w_ref[:, :, columns].reshape(kc, tile),
            preferred_element_type=jnp.float32,
        )
        copy = pltpu.make_async_copy(
            z_tiles.at[j], z_ref.at[:, columns], sems.at[j]
        )
        copy.start()
        copies.append(copy)
    turned[...] = t_full.astype(jnp.float32).T.reshape(turned.shape)
    amp_own[...] = turned[col].astype(amp_own.dtype)
    copy = pltpu.make_async_copy(amp_own, amp_ref, amp_sem)
    copy.start()
    copies.append(copy)
    for copy in copies:
        copy.wait()


def shards(n_row, n_col, t_slab, w_cycle):
    _, panels, share, panel_width = t_slab.shape
    depth, jb = w_cycle.shape
    kc = panels * panel_width
    chips, levels = n_row // CORES, n_col // 2
    anywhere = pl.BlockSpec(memory_space=pl.ANY)
    vmem = pl.BlockSpec(memory_space=pltpu.VMEM)
    dma = pltpu.SemaphoreType.DMA
    t_all, w_all = pl.pallas_call(
        functools.partial(gather_kernel, n_row, n_col, PIECES),
        out_shape=(
            pltpu.VMEM((n_col, share, kc), t_slab.dtype),
            pltpu.VMEM((n_row, depth, jb), w_cycle.dtype),
        ),
        in_specs=[anywhere] * 2,
        out_specs=(vmem, vmem),
        scratch_shapes=[
            pltpu.VMEM(t_slab.shape, t_slab.dtype),
            dma((2,)),
            dma((chips, PIECES)), dma((chips, PIECES)),
            dma((chips, PIECES)), dma((chips, PIECES)),
            dma((levels,)), dma((levels,)),
            dma((levels,)), dma((levels,)),
        ],
        compiler_params=pltpu.CompilerParams(
            collective_id=0, has_side_effects=True
        ),
        name="gather",
    )(t_slab, w_cycle)
    rows = n_col * share
    amp, z = pl.pallas_call(
        product_kernel,
        out_shape=(
            jax.ShapeDtypeStruct((kc // n_col, rows), t_slab.dtype),
            jax.ShapeDtypeStruct((rows, jb), jnp.float32),
        ),
        in_specs=[vmem] * 2,
        out_specs=(anywhere, anywhere),
        scratch_shapes=[
            pltpu.VMEM((jb // TILE, rows, TILE), jnp.float32),
            pltpu.VMEM((n_col, kc // n_col, rows), jnp.float32),
            pltpu.VMEM((kc // n_col, rows), t_slab.dtype),
            dma((jb // TILE,)),
            dma,
        ],
        compiler_params=pltpu.CompilerParams(vmem_limit_bytes=32 * 2**20),
        name="product",
    )(t_all, w_all)
    return amp.T, z


def solution(mesh):
    placed = (P("row", None, "col", None), P("row", "col"))
    return jax.shard_map(
        functools.partial(shards, mesh.shape["row"], mesh.shape["col"]),
        mesh=mesh,
        in_specs=placed,
        out_specs=(P("row", "col"), P("row", "col")),
        check_vma=False,
    )
```

time: 51.2 us -> 16.6 us (0.32)
  blocking collectives: 38.4 us -> 0 us
  Pallas kernels: 0 us -> 15.8 us
  starting transfers between devices: 7.28 us -> 0 us
  matrix products: 2.74 us -> 0 us
  local copies, waits for them, and re-layouts: 1.77 us -> 0 us
    all_gather x2 -> x0, blocking collectives: 38.4 us -> none  [the longest x1 31.1 us: shards(): t_full = lax.all_gather(t_tile, 'col', axis=1, tiled=True)]
    pallas_call x0 -> x2, Pallas kernels: none -> 15.8 us  [the longest x1 13.4 us: shards(): pl.pallas_call(functools.partial(gather_kernel, n_row, n_col, PIECES), ou...]
    all_to_all x1 -> x0, starting transfers between devices: 7.28 us -> none  [shards(): lax.all_to_all(local_rows, 'col', split_axis=1, concat_axis=0, tiled=True)]
    dot_general x1 -> x0, matrix products: 2.74 us -> none  [shards(): cycle_z = jnp.dot(t_full, w_full, preferred_element_type=jnp.float32)]
    unnamed x5 -> x0, local copies, waits for them, and re-layouts: 1.65 us -> none
  transfers between devices with their start and end apart: 1 -> 0, of which waited for: 0 -> 0; matrix products, arithmetic and copies ran while one was open for 0% -> 0% of each run, Pallas kernels for 0% -> 0%
where the time goes in v1:
time: 16.6 us; the launch traced here: 16.4 us
  Pallas kernels  15.8 us (95%)
  between operations  0.64 us (4%)
    pallas_call x1, Pallas kernels, shards(): pl.pallas_call(functools.partial(gather_kernel, n_row, n_col, PIECES), ou...  13.4 us
    pallas_call x1, Pallas kernels, shards(): pl.pallas_call(product_kernel, out_shape=(jax.ShapeDtypeStruct((kc // n_c...  2.37 us

profile of v1, /device:TPU:0, one launch (start us, length us, event | category | flops | bytes accessed | tf_op | source)
XLA Modules:
  0.0 16.4 jit_solution(4839441833675270722)
XLA Ops:
  0.6 13.4 %gather.1 = (bf16[8,64,128]{2,1,0:T(8,128)(2,1)S(1)}, bf16[4,32,2048]{2,1,0:T(8,128)(2,1)S(1)}) custom-call(bf16[1,2,64,64]{3,2,1,0:T(8,128)(2,1)} %t_ref.1, bf16[32,2048]{1,0:T(8,128)(2,1)} %w_ref.1), custom_call_target="tpu_custom_call" | custom-call | tf_op jit(solution)/shard_map/gather/pallas_call | solution.py:165
  14.0 2.4 %product.1 = (bf16[16,512]{1,0:T(8,128)(2,1)}, f32[512,2048]{1,0:T(8,128)}) custom-call(bf16[8,64,128]{2,1,0:T(8,128)(2,1)S(1)} %get-tuple-element.6.t_ref, bf16[4,32,2048]{2,1,0:T(8,128)(2,1)S(1)} %get-tuple-element.7.w_ref), custom_call_target="tpu_custom_call" | custom-call | tf_op jit(solution)/shard_map/product/pallas_call | solution.py:187

commit v2 on v1

v2 whole, which is shorter than its diff:
```python
import functools

import jax
import jax.numpy as jnp
from jax import lax
from jax.experimental import pallas as pl
from jax.experimental.pallas import tpu as pltpu
from jax.sharding import PartitionSpec as P

PIECES = 2
DIRECT = 1
TILE = 256
CORES = 2


def gather_kernel(
    n_row, n_col, t_ref, w_ref, t_all, w_all, t_in, local_sem,
    chip_send, chip_recv, core_send, core_recv, twin_send, twin_recv, t_send, t_recv,
):
    row, col = lax.axis_index("row"), lax.axis_index("col")
    chips, core = n_row // CORES, lax.rem(row, CORES)
    chip = row // CORES
    pieces = chip_send.shape[1]
    kc = t_all.shape[2]
    width = w_ref.shape[1] // pieces
    relayed = pieces - DIRECT

    barrier = pltpu.get_barrier_semaphore()
    for k in range(1, n_row):
        pl.semaphore_signal(
            barrier, inc=1, device_id={"row": lax.rem(row + k, n_row), "col": col}
        )
    for k in range(1, n_col):
        pl.semaphore_signal(
            barrier, inc=1, device_id={"row": row, "col": lax.rem(col + k, n_col)}
        )
    t_stage = pltpu.make_async_copy(t_ref, t_in, local_sem.at[0])
    t_stage.start()
    w_stage = pltpu.make_async_copy(w_ref, w_all.at[row], local_sem.at[1])
    w_stage.start()

    def chip_at(k):
        return lax.rem(chip + k + chips, chips)

    def columns(j):
        return pl.ds(j * width, width)

    def to_chip(k, j):
        return pltpu.make_async_remote_copy(
            src_ref=w_ref.at[:, columns(j)],
            dst_ref=w_all.at[row, :, columns(j)],
            send_sem=chip_send.at[k, j],
            recv_sem=chip_recv.at[k, j],
            device_id={"row": chip_at(k) * CORES + core, "col": col},
        )

    def to_twin(k, j):
        return pltpu.make_async_remote_copy(
            src_ref=w_ref.at[:, columns(j)],
            dst_ref=w_all.at[row, :, columns(j)],
            send_sem=twin_send.at[k, j - relayed],
            recv_sem=twin_recv.at[k, j - relayed],
            device_id={"row": chip_at(k) * CORES + 1 - core, "col": col},
        )

    def to_core(k, j):
        slot = chip_at(-k) * CORES + core
        source = w_ref if k == 0 else w_all.at[slot]
        return pltpu.make_async_remote_copy(
            src_ref=source.at[:, columns(j)],
            dst_ref=w_all.at[slot, :, columns(j)],
            send_sem=core_send.at[k, j],
            recv_sem=core_recv.at[k, j],
            device_id={"row": chip * CORES + 1 - core, "col": col},
        )

    def t_to(k):
        return pltpu.make_async_remote_copy(
            src_ref=t_all.at[col],
            dst_ref=t_all.at[col],
            send_sem=t_send.at[k],
            recv_sem=t_recv.at[k],
            device_id={"row": row, "col": lax.rem(col + k, n_col)},
        )

    others = range(1, chips)
    pl.semaphore_wait(barrier, n_row + n_col - 2)
    for j in range(pieces):
        for k in others:
            to_chip(k, j).start()
            if j >= relayed:
                to_twin(k, j).start()
    t_stage.wait()
    t_all[col] = jnp.concatenate(
        [t_in[0, k] for k in range(t_in.shape[1])], axis=1
    )
    for k in range(1, n_col):
        t_to(k).start()
    for j in range(pieces):
        to_core(0, j).start()

    for j in range(relayed):
        for k in others:
            to_chip(k, j).wait_recv()
            to_core(k, j).start()
    w_stage.wait()
    for k in range(1, n_col):
        t_to(k).wait_recv()
    for j in range(pieces):
        to_core(0, j).wait_recv()
        for k in others:
            if j < relayed:
                to_core(k, j).wait_recv()
            else:
                to_chip(k, j).wait_recv()
                to_twin(k, j).wait_recv()

    for k in range(1, n_col):
        t_to(k).wait_send()
    for j in range(pieces):
        to_core(0, j).wait_send()
        for k in others:
            to_chip(k, j).wait_send()
            if j < relayed:
                to_core(k, j).wait_send()
            else:
                to_twin(k, j).wait_send()


def product_kernel(t_ref, w_ref, amp_ref, z_ref, z_tiles, turned, amp_own, sems, amp_sem):
    col = lax.axis_index("col")
    tile = z_tiles.shape[2]
    kc = t_ref.shape[2]
    t_full = t_ref[...].reshape(-1, kc)
    copies = []
    for j in range(z_tiles.shape[0]):
        columns = pl.ds(j * tile, tile)
        z_tiles[j] = jnp.dot(
            t_full,
            w_ref[:, :, columns].reshape(kc, tile),
            preferred_element_type=jnp.float32,
        )
        copy = pltpu.make_async_copy(
            z_tiles.at[j], z_ref.at[:, columns], sems.at[j]
        )
        copy.start()
        copies.append(copy)
    turned[...] = t_full.astype(jnp.float32).T.reshape(turned.shape)
    amp_own[...] = turned[col].astype(amp_own.dtype)
    copy = pltpu.make_async_copy(amp_own, amp_ref, amp_sem)
    copy.start()
    copies.append(copy)
    for copy in copies:
        copy.wait()


def shards(n_row, n_col, t_slab, w_cycle):
    _, panels, share, panel_width = t_slab.shape
    depth, jb = w_cycle.shape
    kc, rows, chips = panels * panel_width, n_col * share, n_row // CORES
    hbm = pl.BlockSpec(memory_space=pltpu.HBM)
    vmem = pl.BlockSpec(memory_space=pltpu.VMEM)
    dma = pltpu.SemaphoreType.DMA
    t_all, w_all = pl.pallas_call(
        functools.partial(gather_kernel, n_row, n_col),
        out_shape=(
            pltpu.VMEM((n_col, share, kc), t_slab.dtype),
            pltpu.VMEM((n_row, depth, jb), w_cycle.dtype),
        ),
        in_specs=[hbm] * 2,
        out_specs=(vmem, vmem),
        scratch_shapes=[
            pltpu.VMEM(t_slab.shape, t_slab.dtype),
            dma((2,)),
            dma((chips, PIECES)), dma((chips, PIECES)),
            dma((chips, PIECES)), dma((chips, PIECES)),
            dma((chips, max(DIRECT, 1))), dma((chips, max(DIRECT, 1))),
            dma((n_col,)), dma((n_col,)),
        ],
        compiler_params=pltpu.CompilerParams(
            collective_id=0, has_side_effects=True
        ),
        name="gather",
    )(t_slab, w_cycle)
    amp, z = pl.pallas_call(
        product_kernel,
        out_shape=(
            jax.ShapeDtypeStruct((kc // n_col, rows), t_slab.dtype),
            jax.ShapeDtypeStruct((rows, jb), jnp.float32),
        ),
        in_specs=[vmem] * 2,
        out_specs=(hbm, hbm),
        scratch_shapes=[
            pltpu.VMEM((jb // TILE, rows, TILE), jnp.float32),
            pltpu.VMEM((n_col, kc // n_col, rows), jnp.float32),
            pltpu.VMEM((kc // n_col, rows), t_slab.dtype),
            dma((jb // TILE,)),
            dma,
        ],
        compiler_params=pltpu.CompilerParams(vmem_limit_bytes=32 * 2**20),
        name="product",
    )(t_all, w_all)
    return amp.T, z


def solution(mesh):
    placed = (P("row", None, "col", None), P("row", "col"))
    return jax.shard_map(
        functools.partial(shards, mesh.shape["row"], mesh.shape["col"]),
        mesh=mesh,
        in_specs=placed,
        out_specs=(P("row", "col"), P("row", "col")),
        check_vma=False,
    )
```

time: 16.6 us -> 15.3 us (0.922)
  Pallas kernels: 15.8 us -> 14.4 us
    pallas_call x1, Pallas kernels: 13.4 us -> 12.1 us  [shards(): pl.pallas_call(functools.partial(gather_kernel, n_row, n_col), out_shape=...]
where the time goes in v2:
time: 15.3 us; the launch traced here: 15.1 us
  Pallas kernels  14.4 us (94%)
  between operations  0.64 us (4%)
    pallas_call x1, Pallas kernels, shards(): pl.pallas_call(functools.partial(gather_kernel, n_row, n_col), out_shape=...  12.1 us
    pallas_call x1, Pallas kernels, shards(): pl.pallas_call(product_kernel, out_shape=(jax.ShapeDtypeStruct((kc // n_c...  2.37 us

profile of v2, /device:TPU:0, one launch (start us, length us, event | category | flops | bytes accessed | tf_op | source)
XLA Modules:
  0.0 15.1 jit_solution(16992031876902448467)
XLA Ops:
  0.6 12.1 %gather.1 = (bf16[8,64,128]{2,1,0:T(8,128)(2,1)S(1)}, bf16[4,32,2048]{2,1,0:T(8,128)(2,1)S(1)}) custom-call(bf16[1,2,64,64]{3,2,1,0:T(8,128)(2,1)} %t_ref.1, bf16[32,2048]{1,0:T(8,128)(2,1)} %w_ref.1), custom_call_target="tpu_custom_call" | custom-call | tf_op jit(solution)/shard_map/gather/pallas_call | solution.py:164
  12.7 2.4 %product.1 = (bf16[16,512]{1,0:T(8,128)(2,1)}, f32[512,2048]{1,0:T(8,128)}) custom-call(bf16[8,64,128]{2,1,0:T(8,128)(2,1)S(1)} %get-tuple-element.6.t_ref, bf16[4,32,2048]{2,1,0:T(8,128)(2,1)S(1)} %get-tuple-element.7.w_ref), custom_call_target="tpu_custom_call" | custom-call | tf_op jit(solution)/shard_map/product/pallas_call | solution.py:185

commit v3 on v2

--- a/solution.py
+++ b/solution.py
@@ -7,29 +7,32 @@
 from jax.experimental.pallas import tpu as pltpu
 from jax.sharding import PartitionSpec as P
 
-PIECES = 2
-DIRECT = 1
+CUTS = (0, 5, 8)
+PIECES = len(CUTS) - 1
 TILE = 256
 CORES = 2
 
 
 def gather_kernel(
     n_row, n_col, t_ref, w_ref, t_all, w_all, t_in, local_sem,
-    chip_send, chip_recv, core_send, core_recv, twin_send, twin_recv, t_send, t_recv,
+    chip_send, chip_recv, core_send, core_recv, t_send, t_recv,
 ):
     row, col = lax.axis_index("row"), lax.axis_index("col")
     chips, core = n_row // CORES, lax.rem(row, CORES)
     chip = row // CORES
     pieces = chip_send.shape[1]
     kc = t_all.shape[2]
-    width = w_ref.shape[1] // pieces
-    relayed = pieces - DIRECT
+    unit = w_ref.shape[1] // CUTS[-1]
 
     barrier = pltpu.get_barrier_semaphore()
-    for k in range(1, n_row):
+    for k in range(1, chips):
         pl.semaphore_signal(
-            barrier, inc=1, device_id={"row": lax.rem(row + k, n_row), "col": col}
+            barrier, inc=1,
+            device_id={"row": lax.rem(row + k * CORES, n_row), "col": col},
         )
+    pl.semaphore_signal(
+        barrier, inc=1, device_id={"row": chip * CORES + 1 - core, "col": col}
+    )
     for k in range(1, n_col):
         pl.semaphore_signal(
             barrier, inc=1, device_id={"row": row, "col": lax.rem(col + k, n_col)}
@@ -43,31 +46,21 @@
         return lax.rem(chip + k + chips, chips)
 
     def columns(j):
-        return pl.ds(j * width, width)
+        return pl.ds(CUTS[j] * unit, (CUTS[j + 1] - CUTS[j]) * unit)
 
     def to_chip(k, j):
         return pltpu.make_async_remote_copy(
-            src_ref=w_ref.at[:, columns(j)],
+            src_ref=w_all.at[row, :, columns(j)],
             dst_ref=w_all.at[row, :, columns(j)],
             send_sem=chip_send.at[k, j],
             recv_sem=chip_recv.at[k, j],
             device_id={"row": chip_at(k) * CORES + core, "col": col},
         )
 
-    def to_twin(k, j):
-        return pltpu.make_async_remote_copy(
-            src_ref=w_ref.at[:, columns(j)],
-            dst_ref=w_all.at[row, :, columns(j)],
-            send_sem=twin_send.at[k, j - relayed],
-            recv_sem=twin_recv.at[k, j - relayed],
-            device_id={"row": chip_at(k) * CORES + 1 - core, "col": col},
-        )
-
     def to_core(k, j):
         slot = chip_at(-k) * CORES + core
-        source = w_ref if k == 0 else w_all.at[slot]
         return pltpu.make_async_remote_copy(
-            src_ref=source.at[:, columns(j)],
+            src_ref=w_all.at[slot, :, columns(j)],
             dst_ref=w_all.at[slot, :, columns(j)],
             send_sem=core_send.at[k, j],
             recv_sem=core_recv.at[k, j],
@@ -84,36 +77,30 @@
         )
 
     others = range(1, chips)
-    pl.semaphore_wait(barrier, n_row + n_col - 2)
+    pl.semaphore_wait(barrier, chips + n_col - 1)
+    w_stage.wait()
+    for j in range(pieces):
+        to_core(0, j).start()
     for j in range(pieces):
         for k in others:
             to_chip(k, j).start()
-            if j >= relayed:
-                to_twin(k, j).start()
     t_stage.wait()
     t_all[col] = jnp.concatenate(
         [t_in[0, k] for k in range(t_in.shape[1])], axis=1
     )
     for k in range(1, n_col):
         t_to(k).start()
+
     for j in range(pieces):
-        to_core(0, j).start()
-
-    for j in range(relayed):
         for k in others:
             to_chip(k, j).wait_recv()
             to_core(k, j).start()
-    w_stage.wait()
     for k in range(1, n_col):
         t_to(k).wait_recv()
     for j in range(pieces):
         to_core(0, j).wait_recv()
         for k in others:
-            if j < relayed:
-                to_core(k, j).wait_recv()
-            else:
-                to_chip(k, j).wait_recv()
-                to_twin(k, j).wait_recv()
+            to_core(k, j).wait_recv()
 
     for k in range(1, n_col):
         t_to(k).wait_send()
@@ -121,10 +108,7 @@
         to_core(0, j).wait_send()
         for k in others:
             to_chip(k, j).wait_send()
-            if j < relayed:
-                to_core(k, j).wait_send()
-            else:
-                to_twin(k, j).wait_send()
+            to_core(k, j).wait_send()
 
 
 def product_kernel(t_ref, w_ref, amp_ref, z_ref, z_tiles, turned, amp_own, sems, amp_sem):
@@ -174,7 +158,6 @@
             dma((2,)),
             dma((chips, PIECES)), dma((chips, PIECES)),
             dma((chips, PIECES)), dma((chips, PIECES)),
-            dma((chips, max(DIRECT, 1))), dma((chips, max(DIRECT, 1))),
             dma((n_col,)), dma((n_col,)),
         ],
         compiler_params=pltpu.CompilerParams(

time: 15.3 us -> 15.1 us (0.987)
  no operation moved by 1% of the time
where the time goes in v3:
time: 15.1 us; the launch traced here: 15 us
  Pallas kernels  14.3 us (95%)
  between operations  0.64 us (4%)
    pallas_call x1, Pallas kernels, shards(): pl.pallas_call(functools.partial(gather_kernel, n_row, n_col), out_shape=...  12 us
    pallas_call x1, Pallas kernels, shards(): pl.pallas_call(product_kernel, out_shape=(jax.ShapeDtypeStruct((kc // n_c...  2.37 us

profile of v3, /device:TPU:0, one launch (start us, length us, event | category | flops | bytes accessed | tf_op | source)
XLA Modules:
  0.0 15.0 jit_solution(13156128885275904682)
XLA Ops:
  0.6 12.0 %gather.1 = (bf16[8,64,128]{2,1,0:T(8,128)(2,1)S(1)}, bf16[4,32,2048]{2,1,0:T(8,128)(2,1)S(1)}) custom-call(bf16[1,2,64,64]{3,2,1,0:T(8,128)(2,1)} %t_ref.1, bf16[32,2048]{1,0:T(8,128)(2,1)} %w_ref.1), custom_call_target="tpu_custom_call" | custom-call | tf_op jit(solution)/shard_map/gather/pallas_call | solution.py:148
  12.6 2.4 %product.1 = (bf16[16,512]{1,0:T(8,128)(2,1)}, f32[512,2048]{1,0:T(8,128)}) custom-call(bf16[8,64,128]{2,1,0:T(8,128)(2,1)S(1)} %get-tuple-element.6.t_ref, bf16[4,32,2048]{2,1,0:T(8,128)(2,1)S(1)} %get-tuple-element.7.w_ref), custom_call_target="tpu_custom_call" | custom-call | tf_op jit(solution)/shard_map/product/pallas_call | solution.py:168

commit v4 on v3

--- a/solution.py
+++ b/solution.py
@@ -25,6 +25,10 @@
     unit = w_ref.shape[1] // CUTS[-1]
 
     barrier = pltpu.get_barrier_semaphore()
+    for k in range(1, n_col):
+        pl.semaphore_signal(
+            barrier, inc=1, device_id={"row": row, "col": lax.rem(col + k, n_col)}
+        )
     for k in range(1, chips):
         pl.semaphore_signal(
             barrier, inc=1,
@@ -33,10 +37,6 @@
     pl.semaphore_signal(
         barrier, inc=1, device_id={"row": chip * CORES + 1 - core, "col": col}
     )
-    for k in range(1, n_col):
-        pl.semaphore_signal(
-            barrier, inc=1, device_id={"row": row, "col": lax.rem(col + k, n_col)}
-        )
     t_stage = pltpu.make_async_copy(t_ref, t_in, local_sem.at[0])
     t_stage.start()
     w_stage = pltpu.make_async_copy(w_ref, w_all.at[row], local_sem.at[1])

time: 15.1 us -> 15.1 us (level)
  no operation moved by 1% of the time
where the time goes in v4:
time: 15.1 us; the launch traced here: 14.9 us
  Pallas kernels  14.3 us (95%)
  between operations  0.64 us (4%)
    pallas_call x1, Pallas kernels, shards(): pl.pallas_call(functools.partial(gather_kernel, n_row, n_col), out_shape=...  11.9 us
    pallas_call x1, Pallas kernels, shards(): pl.pallas_call(product_kernel, out_shape=(jax.ShapeDtypeStruct((kc // n_c...  2.37 us

profile of v4, /device:TPU:0, one launch (start us, length us, event | category | flops | bytes accessed | tf_op | source)
XLA Modules:
  0.0 14.9 jit_solution(679615150091942657)
XLA Ops:
  0.6 11.9 %gather.1 = (bf16[8,64,128]{2,1,0:T(8,128)(2,1)S(1)}, bf16[4,32,2048]{2,1,0:T(8,128)(2,1)S(1)}) custom-call(bf16[1,2,64,64]{3,2,1,0:T(8,128)(2,1)} %t_ref.1, bf16[32,2048]{1,0:T(8,128)(2,1)} %w_ref.1), custom_call_target="tpu_custom_call" | custom-call | tf_op jit(solution)/shard_map/gather/pallas_call | solution.py:148
  12.6 2.4 %product.1 = (bf16[16,512]{1,0:T(8,128)(2,1)}, f32[512,2048]{1,0:T(8,128)}) custom-call(bf16[8,64,128]{2,1,0:T(8,128)(2,1)S(1)} %get-tuple-element.6.t_ref, bf16[4,32,2048]{2,1,0:T(8,128)(2,1)S(1)} %get-tuple-element.7.w_ref), custom_call_target="tpu_custom_call" | custom-call | tf_op jit(solution)/shard_map/product/pallas_call | solution.py:168

commit v5 on v4

--- a/solution.py
+++ b/solution.py
@@ -7,7 +7,7 @@
 from jax.experimental.pallas import tpu as pltpu
 from jax.sharding import PartitionSpec as P
 
-CUTS = (0, 5, 8)
+CUTS = (0, 8)
 PIECES = len(CUTS) - 1
 TILE = 256
 CORES = 2

time: 15.1 us -> 15.1 us (level)
  no operation moved by 1% of the time
where the time goes in v5:
time: 15.1 us; the launch traced here: 15 us
  Pallas kernels  14.3 us (95%)
  between operations  0.64 us (4%)
    pallas_call x1, Pallas kernels, shards(): pl.pallas_call(functools.partial(gather_kernel, n_row, n_col), out_shape=...  12 us
    pallas_call x1, Pallas kernels, shards(): pl.pallas_call(product_kernel, out_shape=(jax.ShapeDtypeStruct((kc // n_c...  2.37 us

profile of v5, /device:TPU:0, one launch (start us, length us, event | category | flops | bytes accessed | tf_op | source)
XLA Modules:
  0.0 15.0 jit_solution(11269256903843726015)
XLA Ops:
  0.6 12.0 %gather.1 = (bf16[8,64,128]{2,1,0:T(8,128)(2,1)S(1)}, bf16[4,32,2048]{2,1,0:T(8,128)(2,1)S(1)}) custom-call(bf16[1,2,64,64]{3,2,1,0:T(8,128)(2,1)} %t_ref.1, bf16[32,2048]{1,0:T(8,128)(2,1)} %w_ref.1), custom_call_target="tpu_custom_call" | custom-call | tf_op jit(solution)/shard_map/gather/pallas_call | solution.py:148
  12.6 2.4 %product.1 = (bf16[16,512]{1,0:T(8,128)(2,1)}, f32[512,2048]{1,0:T(8,128)}) custom-call(bf16[8,64,128]{2,1,0:T(8,128)(2,1)S(1)} %get-tuple-element.6.t_ref, bf16[4,32,2048]{2,1,0:T(8,128)(2,1)S(1)} %get-tuple-element.7.w_ref), custom_call_target="tpu_custom_call" | custom-call | tf_op jit(solution)/shard_map/product/pallas_call | solution.py:168
